TPU v7x, 32 devices: a whole 2x2x4 slice. The times are simulated.
32 devices in a mesh: node: 8 (over y, x, core), local: 4 (over z).
Axes of the slice: x: 2, y: 2, z: 4, core: 2. Of those that a mesh axis runs over, the one named last changes fastest.
Arguments:
- upstream: bfloat16 [256, 12800], P(('node', 'local')), may hold values from -1.5 to 1.5
- block_image: int32 [64], replicated, may hold values from 0 to 15, as said below
- image_owner: int32 [16], replicated, may hold values from 0 to 7, as said below
- vision_out: bfloat16 [24, 4, 12800], P('node', 'local'), may hold values from -200 to 200
- norm_gain: float32 [12800], replicated, may hold values from 0.5 to 2
- layer_scale: float32 [3200], replicated, may hold values from 0.5 to 2
- down_weight: bfloat16 [3200, 2144], P(None, 'local'), may hold values from -0.125 to 0.125
- hidden_pre: bfloat16 [24, 16, 2144], P('node', None, 'local'), may hold values from -6 to 6
Outputs:
- hidden_grad: bfloat16 [24, 16, 2144], P('node', None, 'local')
- down_grad: float32 [3200, 2144], P('node', 'local')
- norm_grads: float32 [2, 12800], replicated
Inputs may be any that keep to these rules, and one draw needn't show every extreme that they name: `block_image`: within one node's blocks, images with the same owner are the same image, so a node reads at most one image of each owner; an image may be read by several blocks of a node and by several nodes. `image_owner`: every node owns at least one image and at most 3, and some node owns exactly 3.
All inputs are finite; a program needn't handle non-finite values.
Results may differ from a plain program's by a relative error of at most 0.0057.
Values may be sent and summed in bfloat16 or wider, within the bound.
A program may use at most 64 MiB of HBM per device.

v0:
```python
import jax
import jax.numpy as jnp
from jax import lax
from jax.sharding import PartitionSpec as P

epsilon = 1e-06
half_root = 0.7071067811865476
inv_root_two_pi = 0.3989422804014327


def gelu_parts(preact):
    normal_cdf = 0.5 * (1.0 + jax.scipy.special.erf(preact * half_root))
    density = jnp.exp(-0.5 * preact * preact) * inv_root_two_pi
    return (preact * normal_cdf, normal_cdf + preact * density)


def owner_ranks(image_owner):
    positions = jnp.arange(image_owner.shape[0], dtype=jnp.int32)
    same_owner = (image_owner[:, None] == image_owner[None, :]) & (
        positions[None, :] < positions[:, None]
    )
    return jnp.sum(same_owner.astype(jnp.int32), axis=1)


def flat_norms(norm_terms):
    return lax.psum(norm_terms, ("node", "local"))


def body(
    upstream, block_image, image_owner, vision_out, norm_gain, layer_scale, down_weight, hidden_pre
):
    local_count = lax.axis_size("local")
    node_count = lax.axis_size("node")
    width_in = upstream.shape[1]
    model_width = layer_scale.shape[0]
    merge_count = width_in // model_width
    blocks_here = upstream.shape[0] // local_count
    node_blocks = local_count * blocks_here
    image_count = image_owner.shape[0]
    own_cap = vision_out.shape[0]
    unit_count = down_weight.shape[1]
    node_index = lax.axis_index("node")
    by_block = upstream.reshape(blocks_here, local_count, width_in)
    position_rows = lax.all_to_all(
        by_block, "local", split_axis=1, concat_axis=0, tiled=True
    ).reshape(node_blocks, width_in)
    image_table = jnp.arange(image_count, dtype=jnp.int32)
    block_match = block_image[:, None] == image_table[None, :]
    block_owner = jnp.sum(jnp.where(block_match, image_owner[None, :], 0), axis=1)
    block_rank = jnp.sum(jnp.where(block_match, owner_ranks(image_owner)[None, :], 0), axis=1)
    owner_table = block_owner.reshape(node_count, node_blocks)
    rank_table = block_rank.reshape(node_count, node_blocks)
    own_owners = lax.dynamic_index_in_dim(owner_table, node_index, 0, keepdims=False)
    node_table = jnp.arange(node_count, dtype=jnp.int32)
    to_owner = (node_table[:, None] == own_owners[None, :]).astype(jnp.bfloat16)
    node_sums = jnp.dot(to_owner, position_rows, preferred_element_type=jnp.float32).astype(
        jnp.bfloat16
    )
    arrived = lax.all_to_all(node_sums, "node", split_axis=0, concat_axis=0, tiled=True)
    from_owner = owner_table == node_index
    source_slot = jnp.max(jnp.where(from_owner, rank_table, -1), axis=1)
    slot_table = jnp.arange(own_cap, dtype=jnp.int32)
    slot_pick = (slot_table[:, None] == source_slot[None, :]).astype(jnp.bfloat16)
    grad_rows = jnp.dot(slot_pick, arrived, preferred_element_type=jnp.float32)
    inputs = vision_out.reshape(own_cap, width_in).astype(jnp.float32)
    average = jnp.mean(inputs, axis=1, keepdims=True)
    centred = inputs - average
    inv_std = lax.rsqrt(jnp.mean(centred * centred, axis=1, keepdims=True) + epsilon)
    normed = centred * inv_std
    scaled = grad_rows * norm_gain
    input_grad = inv_std * (
        scaled
        - jnp.mean(scaled, axis=1, keepdims=True)
        - normed * jnp.mean(scaled * normed, axis=1, keepdims=True)
    )
    norm_terms = jnp.stack([jnp.sum(grad_rows * normed, axis=0), jnp.sum(grad_rows, axis=0)])
    branch = (input_grad.reshape(own_cap, merge_count, model_width) * layer_scale).astype(
        jnp.bfloat16
    )
    patches = lax.all_gather(branch, "local", axis=1, tiled=True)
    patch_rows = patches.reshape(-1, model_width)
    row_count = patch_rows.shape[0]
    preact = hidden_pre.reshape(row_count, unit_count).astype(jnp.float32)
    activation, derivative = gelu_parts(preact)
    hidden_act = activation.astype(jnp.bfloat16)
    shard_rows = model_width // node_count
    hidden_in = jnp.dot(patch_rows, down_weight, preferred_element_type=jnp.float32)
    hidden_grad = (hidden_in * derivative).astype(jnp.bfloat16).reshape(hidden_pre.shape)
    by_column = patch_rows.reshape(row_count, node_count, shard_rows)
    my_columns = lax.all_to_all(by_column, "node", split_axis=1, concat_axis=0, tiled=True).reshape(
        node_count * row_count, shard_rows
    )
    down_grad = lax.dot_general(
        my_columns,
        lax.all_gather(hidden_act, "node", axis=0, tiled=True),
        (((0,), (0,)), ((), ())),
        preferred_element_type=jnp.float32,
    )
    norm_grads = flat_norms(norm_terms)
    return (hidden_grad, down_grad, norm_grads)


def solution(mesh):
    placed = (
        P(("node", "local"), None),
        P(),
        P(),
        P("node", "local", None),
        P(),
        P(),
        P(None, "local"),
        P("node", None, "local"),
    )
    return jax.shard_map(
        body,
        mesh=mesh,
        in_specs=placed,
        out_specs=(P("node", None, "local"), P("node", "local"), P()),
        check_vma=False,
    )
```

profile of v0, /device:TPU:0, one launch (start us, length us, event | category | flops | bytes accessed | tf_op | source)
XLA Modules:
  0.0 193.4 jit_solution(8986583803455158794)
XLA Ops:
  7.2 0.0 copy-start
  7.2 0.0 copy-start.1
  7.2 1.8 reshape.68
  9.0 1.8 copy.31
  10.8 6.3 %all-to-all-start = ((bf16[2,4,12800]{2,0,1:T(2,128)(2,1)}), bf16[2,4,12800]{2,0,1:T(2,128)(2,1)}, u32[]{:S(2)}, u32[]{:S(2)}) async-start(bf16[2,4,12800]{2,0,1:T(2,128)(2,1)} %copy.31), calls=%async_computation | async-start | bytes 409600 | tf_op jit(solution)/shard_map/all_to_all | solution.py:44
  17.1 0.9 convert_reduce_fusion.1
  18.0 1.1 convert_reduce_fusion
  19.1 0.8 select_reduce_fusion
  19.9 0.1 reshape.67
  20.0 0.1 reshape.66
  20.0 0.1 select_reduce_fusion.2
  20.2 1.5 fusion.22
  21.7 10.9 %all_gather.7 = bf16[384,536]{1,0:T(8,128)(2,1)} all-gather(bf16[48,536]{1,0:T(8,128)(2,1)S(1)} %get-tuple-element.9), channel_id=1, replica_groups=mesh['node'=8,'local'=4] {'node'}, dimensions={0}, use_global_device_ids=true | all-gather | bytes 463104 | tf_op jit(solution)/shard_map/all_gather | solution.py:95
  32.6 1.2 fusion.12
  33.8 0.0 all-to-all-done
  33.8 1.7 reshape.69
  35.5 1.8 fusion
  37.3 0.5 broadcast.49
  37.8 2.3 %reduce.1 = bf16[8,12800]{1,0:T(8,128)(2,1)} reduce(bf16[8,1,12800]{2,0,1:T(8,128)(2,1)} %fusion, bf16[]{:T(256)} %broadcast.49), dimensions={1}, to_apply=%copy.32.reduce_sub_computation | reduce | bytes 409602 | tf_op jit(solution)/shard_map/all_to_all | solution.py:59
  40.1 1.7 reshape.75
  41.8 4.0 %all-to-all-start.1 = ((bf16[8,2,6400]{2,1,0:T(2,128)(2,1)}), bf16[8,2,6400]{2,1,0:T(2,128)(2,1)}, u32[]{:S(2)}, u32[]{:S(2)}) async-start(bf16[8,2,6400]{2,1,0:T(2,128)(2,1)} %reshape.75), calls=%async_computation.1 | async-start | bytes 409600 | tf_op jit(solution)/shard_map/all_to_all | solution.py:59
  45.8 0.0 all-reduce.2.cloned.1.call-start
  45.9 6.3 %all-to-all-done.1 = bf16[8,2,6400]{2,1,0:T(2,128)(2,1)} async-done(((bf16[8,2,6400]{2,1,0:T(2,128)(2,1)}), bf16[8,2,6400]{2,1,0:T(2,128)(2,1)}, u32[]{:S(2)}, u32[]{:S(2)}) %all-to-all-start.1) | async-done | bytes 204832 | tf_op jit(solution)/shard_map/all_to_all | solution.py:59
  52.1 2.2 %reshape.76 = bf16[8,1,12800]{2,1,0:T(2,128)(2,1)} reshape(bf16[8,2,6400]{2,1,0:T(2,128)(2,1)} %all-to-all-done.1) | data formatting | bytes 409600
  54.4 0.0 copy-done.1
  54.4 2.1 %fusion.11 = (f32[12800]{0:T(1024)S(1)}, f32[3]{0:T(128)S(1)}, f32[3]{0:T(128)S(1)}, f32[12800]{0:T(1024)}, f32[3,12800]{1,0:T(4,128)S(1)}) fusion(bf16[3,1,12800]{2,0,1:T(4,128)(2,1)S(1)} %copy-done.1, f32[3]{0:T(128)S(1)} %add_rsqrt_fusion, f32[3]{0:T(128)S(1)} %broadcast_multiply_fusion.2, f32[12800]{0:T(1024)} %param.12, ...), kind=kOutput, calls=%fused_computation.20 | convolution fusion | flops 972818 | bytes 588880 | tf_op jit(solution)/shard_map/dot_general | solution.py:64
  56.5 0.6 stack.9
  57.1 1.7 fusion.10
  58.8 0.0 copy-start.2
  58.8 1.7 reshape.70
  60.5 0.9 multiply_convert_fusion
  61.5 0.7 copy.33
  62.2 0.8 stack.10
  63.0 1.5 pad_maximum_fusion
  64.6 0.0 all-reduce.2.cloned.1.call-update
  64.6 15.3 %all_gather.6 = bf16[3,16,3200]{2,0,1:T(4,128)(2,1)S(1)} all-gather(bf16[3,4,3200]{2,0,1:T(4,128)(2,1)} %copy.33), channel_id=1, replica_groups=mesh['node'=8,'local'=4] {'local'}, dimensions={1}, use_global_device_ids=true | all-gather | bytes 384000 | tf_op jit(solution)/shard_map/all_gather | solution.py:80
  79.9 0.8 copy.34
  80.7 2.6 %reshape_reshape.3 = bf16[48,8,400]{2,1,0:T(8,128)(2,1)} reshape(bf16[3,16,3200]{2,1,0:T(8,128)(2,1)} %copy.34) | data formatting | bytes 614400 | tf_op jit(solution)/shard_map/reshape;reshape | solution.py:89
  83.3 1.9 copy.36
  85.2 4.1 %all-to-all-start.2 = ((bf16[48,8,400]{2,0,1:T(8,128)(2,1)}), bf16[48,8,400]{2,0,1:T(8,128)(2,1)}, u32[]{:S(2)}, u32[]{:S(2)}) async-start(bf16[48,8,400]{2,0,1:T(8,128)(2,1)} %copy.36), calls=%async_computation.2 | async-start | bytes 786432 | tf_op jit(solution)/shard_map/all_to_all | solution.py:90
  89.3 0.0 copy-done
  89.3 0.0 copy-done.2
  89.3 2.7 %fusion.1 = bf16[48,536]{1,0:T(8,128)(2,1)} fusion(bf16[48,3200]{1,0:T(8,128)(2,1)} %bitcast.55, bf16[3200,536]{0,1:T(8,128)(2,1)S(1)} %copy-done, f32[48,536]{1,0:T(8,128)S(1)} %copy-done.2, bf16[48,536]{1,0:T(8,128)(2,1)} %bitcast.56), kind=kOutput, calls=%fused_computation.3 | convolution fusion | flops 164865024 | bytes 3943424 | tf_op jit(solution)/shard_map/dot_general | solution.py:87
  92.0 5.6 %all-to-all-done.2 = bf16[48,8,400]{2,0,1:T(8,128)(2,1)} async-done(((bf16[48,8,400]{2,0,1:T(8,128)(2,1)}), bf16[48,8,400]{2,0,1:T(8,128)(2,1)}, u32[]{:S(2)}, u32[]{:S(2)}) %all-to-all-start.2) | async-done | bytes 307232 | tf_op jit(solution)/shard_map/all_to_all | solution.py:90
  97.6 2.6 %fusion.27 = f32[400,536]{1,0:T(8,128)} fusion(bf16[384,400]{1,0:T(8,128)(2,1)} %bitcast.11, bf16[384,536]{1,0:T(8,128)(2,1)} %all_gather.7), kind=kOutput, calls=%fused_computation.51 | convolution fusion | flops 164659200 | bytes 1576448 | tf_op jit(solution)/shard_map/dot_general | solution.py:93
  100.2 84.8 %all-reduce.2.cloned.1.call-done = f32[2,12800]{1,0:T(2,128)} async-done(((f32[2,12800]{1,0:T(2,128)}), f32[2,12800]{1,0:T(2,128)}) %all-reduce.2.cloned.1.call-update) | async-done | bytes 102416 | tf_op jit(solution)/shard_map/psum | solution.py:26
  185.0 1.5 copy.46
  (4 shorter events, 0.0 us)
Async XLA Ops:
  7.2 82.1 %copy-start = (bf16[3200,536]{0,1:T(8,128)(2,1)S(1)}, bf16[3200,536]{0,1:T(8,128)(2,1)}, u32[]{:S(2)}) copy-start(bf16[3200,536]{0,1:T(8,128)(2,1)} %param.14) | copy-start | bytes 10291204
  7.2 47.2 %copy-start.1 = (bf16[3,1,12800]{2,0,1:T(4,128)(2,1)S(1)}, bf16[3,1,12800]{2,0,1:T(4,128)(2,1)}, u32[]{:S(2)}) copy-start(bf16[3,1,12800]{2,0,1:T(4,128)(2,1)} %param.11) | copy-start | bytes 230404
  10.8 23.0 %all-to-all-start = ((bf16[2,4,12800]{2,0,1:T(2,128)(2,1)}), bf16[2,4,12800]{2,0,1:T(2,128)(2,1)}, u32[]{:S(2)}, u32[]{:S(2)}) async-start(bf16[2,4,12800]{2,0,1:T(2,128)(2,1)} %copy.31), calls=%async_computation | async-start | bytes 409600 | tf_op jit(solution)/shard_map/all_to_all | solution.py:44
  41.8 10.4 %all-to-all-start.1 = ((bf16[8,2,6400]{2,1,0:T(2,128)(2,1)}), bf16[8,2,6400]{2,1,0:T(2,128)(2,1)}, u32[]{:S(2)}, u32[]{:S(2)}) async-start(bf16[8,2,6400]{2,1,0:T(2,128)(2,1)} %reshape.75), calls=%async_computation.1 | async-start | bytes 409600 | tf_op jit(solution)/shard_map/all_to_all | solution.py:59
  45.8 139.2 %all-reduce.2.cloned.1.call-start = ((), (), s32[]{:S(2)}) async-start(), calls=%async_computation.3 | async-start | bytes 204800 | tf_op jit(solution)/shard_map/psum | solution.py:26
  58.8 30.5 %copy-start.2 = (f32[48,536]{1,0:T(8,128)S(1)}, f32[48,536]{1,0:T(8,128)}, u32[]{:S(2)}) copy-start(f32[48,536]{1,0:T(8,128)} %get-tuple-element.10) | copy-start | bytes 308740
  85.2 12.4 %all-to-all-start.2 = ((bf16[48,8,400]{2,0,1:T(8,128)(2,1)}), bf16[48,8,400]{2,0,1:T(8,128)(2,1)}, u32[]{:S(2)}, u32[]{:S(2)}) async-start(bf16[48,8,400]{2,0,1:T(8,128)(2,1)} %copy.36), calls=%async_computation.2 | async-start | bytes 786432 | tf_op jit(solution)/shard_map/all_to_all | solution.py:90
Sparse Core Ops, SparseCore 0:
  64.7 120.2 all-reduce.1
where the time goes:
time: 195 us; the launch traced here: 193 us
  waiting for transfers between devices  96.7 us (50%)
  blocking collectives  26.2 us (13%)
  local copies, waits for them, and re-layouts  20.6 us (11%)
  starting transfers between devices  14.5 us (7%)
  between operations  14.1 us (7%)
  other arithmetic  12.1 us (6%)
  matrix products  9.27 us (5%)
    psum x1, waiting for transfers between devices, flat_norms(): return lax.psum(norm_terms, ('node', 'local'))  84.8 us
    all_gather x1, blocking collectives, body(): patches = lax.all_gather(branch, 'local', axis=1, tiled=True)  15.3 us
    all_gather x1, blocking collectives, body(): lax.all_gather(hidden_act, 'node', axis=0, tiled=True)  10.9 us
    all_to_all x1, starting transfers between devices, body(): lax.all_to_all(by_block, 'local', split_axis=1, concat_axis=0, tiled=True)  6.32 us
    all_to_all x1, waiting for transfers between devices, body(): lax.all_to_all(node_sums, 'node', split_axis=0, concat_axis=0, tiled=True)  6.27 us
    all_to_all x1, waiting for transfers between devices, body(): lax.all_to_all(by_column, 'node', split_axis=1, concat_axis=0, tiled=True)  5.59 us
    unnamed x9, local copies, waits for them, and re-layouts  5.45 us
    another operation x2, local copies, waits for them, and re-layouts, body(): by_column = patch_rows.reshape(row_count, node_count, shard_rows)  4.45 us
  transfers between devices with their start and end apart: 4, of which 3 were waited for; matrix products, arithmetic and copies ran while one was open for 8% of the time, Pallas kernels for 0%

commit v1 on v0

--- a/solution.py
+++ b/solution.py
@@ -23,7 +23,16 @@
 
 
 def flat_norms(norm_terms):
-    return lax.psum(norm_terms, ("node", "local"))
+    axes = ("node", "local")
+    total = lax.axis_size("node") * lax.axis_size("local")
+    width = norm_terms.shape[1]
+    share = -(-width // total)
+    padded = jnp.pad(norm_terms, ((0, 0), (0, share * total - width)))
+    by_share = padded.reshape(2, total, share).transpose(1, 0, 2)
+    terms = lax.all_to_all(by_share, axes, split_axis=0, concat_axis=0, tiled=True)
+    sums = jnp.sum(terms, axis=0)
+    whole = lax.all_gather(sums, axes, axis=0)
+    return whole.transpose(1, 0, 2).reshape(2, total * share)[:, :width]
 
 
 def body(

time: 195 us -> 168 us (0.86)
  waiting for transfers between devices: 96.7 us -> 6.33 us
  blocking collectives: 26.2 us -> 96 us
  between operations: 14.1 us -> 0.74 us
  starting transfers between devices: 14.5 us -> 18.7 us
    psum x1 -> x0, waiting for transfers between devices: 84.8 us -> none  [flat_norms(): return lax.psum(norm_terms, ('node', 'local'))]
    all_gather x0 -> x1, blocking collectives: none -> 70 us  [flat_norms(): whole = lax.all_gather(sums, axes, axis=0)]
    all_to_all x1, waiting for transfers between devices: 5.59 us -> 0.01 us  [body(): lax.all_to_all(by_column, 'node', split_axis=1, concat_axis=0, tiled=True)]
    all_to_all x0 -> x1, starting transfers between devices: none -> 4.32 us  [flat_norms(): lax.all_to_all(by_share, axes, split_axis=0, concat_axis=0, tiled=True)]
    unnamed x9 -> x8, local copies, waits for them, and re-layouts: 5.45 us -> 3.91 us
  transfers between devices with their start and end apart: 4 -> 4, of which waited for: 3 -> 1; matrix products, arithmetic and copies ran while one was open for 8% -> 11% of each run, Pallas kernels for 0% -> 0%
where the time goes in v1:
time: 168 us; the launch traced here: 167 us
  blocking collectives  96 us (57%)
  local copies, waits for them, and re-layouts  22.4 us (13%)
  starting transfers between devices  18.7 us (11%)
  other arithmetic  13.2 us (8%)
  matrix products  9.27 us (6%)
  waiting for transfers between devices  6.33 us (4%)
    all_gather x1, blocking collectives, flat_norms(): whole = lax.all_gather(sums, axes, axis=0)  70 us
    all_gather x1, blocking collectives, body(): patches = lax.all_gather(branch, 'local', axis=1, tiled=True)  15.1 us
    all_gather x1, blocking collectives, body(): lax.all_gather(hidden_act, 'node', axis=0, tiled=True)  10.9 us
    all_to_all x1, waiting for transfers between devices, body(): lax.all_to_all(node_sums, 'node', split_axis=0, concat_axis=0, tiled=True)  6.32 us
    all_to_all x1, starting transfers between devices, body(): lax.all_to_all(by_block, 'local', split_axis=1, concat_axis=0, tiled=True)  6.32 us
    another operation x2, local copies, waits for them, and re-layouts, body(): by_column = patch_rows.reshape(row_count, node_count, shard_rows)  4.45 us
    all_to_all x1, starting transfers between devices, flat_norms(): lax.all_to_all(by_share, axes, split_axis=0, concat_axis=0, tiled=True)  4.32 us
    all_to_all x1, starting transfers between devices, body(): lax.all_to_all(by_column, 'node', split_axis=1, concat_axis=0, tiled=True)  4.09 us
  transfers between devices with their start and end apart: 4, of which 1 were waited for; matrix products, arithmetic and copies ran while one was open for 11% of the time, Pallas kernels for 0%

profile of v1, /device:TPU:0, one launch (start us, length us, event | category | flops | bytes accessed | tf_op | source)
XLA Modules:
  0.0 166.7 jit_solution(1903235775321737324)
XLA Ops:
  0.6 0.0 copy-start
  0.6 0.0 copy-start.1
  0.7 1.8 %reshape.76 = bf16[2,4,12800]{2,1,0:T(4,128)(2,1)} reshape(bf16[8,12800]{1,0:T(8,128)(2,1)} %param.8) | data formatting | bytes 409600 | tf_op jit(solution)/shard_map/reshape | solution.py:52
  2.5 1.8 %copy.33 = bf16[2,4,12800]{2,0,1:T(2,128)(2,1)} copy(bf16[2,4,12800]{2,1,0:T(4,128)(2,1)} %reshape.76) | data formatting | bytes 409600 | tf_op jit(solution)/shard_map/reshape | solution.py:52
  4.3 6.3 %all-to-all-start = ((bf16[2,4,12800]{2,0,1:T(2,128)(2,1)}), bf16[2,4,12800]{2,0,1:T(2,128)(2,1)}, u32[]{:S(2)}, u32[]{:S(2)}) async-start(bf16[2,4,12800]{2,0,1:T(2,128)(2,1)} %copy.33), calls=%async_computation | async-start | bytes 409600 | tf_op jit(solution)/shard_map/all_to_all | solution.py:53
  10.6 0.9 convert_reduce_fusion.1
  11.5 1.1 convert_reduce_fusion
  12.6 0.8 select_reduce_fusion
  13.4 0.1 reshape.75
  13.4 0.1 reshape.74
  13.5 0.1 select_reduce_fusion.2
  13.7 1.5 fusion.22
  15.2 10.9 %all_gather.13 = bf16[384,536]{1,0:T(8,128)(2,1)} all-gather(bf16[48,536]{1,0:T(8,128)(2,1)S(1)} %get-tuple-element.9), channel_id=1, replica_groups=mesh['node'=8,'local'=4] {'node'}, dimensions={0}, use_global_device_ids=true | all-gather | bytes 463104 | tf_op jit(solution)/shard_map/all_gather | solution.py:104
  26.1 1.2 fusion.12
  27.3 0.0 all-to-all-done
  27.3 1.7 %reshape.77 = bf16[8,12800]{1,0:T(8,128)(2,1)} reshape(bf16[4,2,1,12800]{3,1,0,2:T(2,128)(2,1)} %bitcast.3) | data formatting | bytes 409600 | tf_op jit(solution)/shard_map/reshape | solution.py:55
  28.9 1.8 %fusion = bf16[8,1,12800]{2,0,1:T(8,128)(2,1)} fusion(bf16[8,12800]{1,0:T(8,128)(2,1)} %reshape.77, s32[8]{0:T(128)S(1)} %dynamic-slice_bitcast_fusion), kind=kOutput, calls=%fused_computation.1 | convolution fusion | flops 1740864 | bytes 409632 | tf_op jit(solution)/shard_map/dot_general | solution.py:65
  30.8 0.5 broadcast.49
  31.3 2.3 %reduce.1 = bf16[8,12800]{1,0:T(8,128)(2,1)} reduce(bf16[8,1,12800]{2,0,1:T(8,128)(2,1)} %fusion, bf16[]{:T(256)} %broadcast.49), dimensions={1}, to_apply=%copy.34.reduce_sub_computation | reduce | bytes 409602 | tf_op jit(solution)/shard_map/all_to_all | solution.py:68
  33.6 1.7 reshape.88
  35.3 4.0 %all-to-all-start.1 = ((bf16[8,2,6400]{2,1,0:T(2,128)(2,1)}), bf16[8,2,6400]{2,1,0:T(2,128)(2,1)}, u32[]{:S(2)}, u32[]{:S(2)}) async-start(bf16[8,2,6400]{2,1,0:T(2,128)(2,1)} %reshape.88), calls=%async_computation.1 | async-start | bytes 409600 | tf_op jit(solution)/shard_map/all_to_all | solution.py:68
  39.3 6.3 %all-to-all-done.1 = bf16[8,2,6400]{2,1,0:T(2,128)(2,1)} async-done(((bf16[8,2,6400]{2,1,0:T(2,128)(2,1)}), bf16[8,2,6400]{2,1,0:T(2,128)(2,1)}, u32[]{:S(2)}, u32[]{:S(2)}) %all-to-all-start.1) | async-done | bytes 204832 | tf_op jit(solution)/shard_map/all_to_all | solution.py:68
  45.6 2.2 %reshape.89 = bf16[8,1,12800]{2,1,0:T(2,128)(2,1)} reshape(bf16[8,2,6400]{2,1,0:T(2,128)(2,1)} %all-to-all-done.1) | data formatting | bytes 409600
  47.9 0.0 copy-done.1
  47.9 2.1 %fusion.11 = (f32[12800]{0:T(1024)}, f32[3]{0:T(128)S(1)}, f32[3]{0:T(128)S(1)}, f32[12800]{0:T(1024)}, f32[3,12800]{1,0:T(4,128)S(1)}) fusion(bf16[3,1,12800]{2,0,1:T(4,128)(2,1)S(1)} %copy-done.1, f32[3]{0:T(128)S(1)} %add_rsqrt_fusion, f32[3]{0:T(128)S(1)} %broadcast_multiply_fusion.2, f32[12800]{0:T(1024)} %param.12, bf16[8,1,12800]{2,1,0:T(2,128)(2,1)} %reshape.89, ...), kind=kOutput, calls=%fused_computation.20 | convolution fusion | flops 972818 | bytes 588880 | tf_op jit(solution)/shard_map/dot_general | solution.py:73
  50.0 1.7 fusion.10
  51.6 0.0 copy-start.2
  51.6 1.7 %reshape.78 = f32[3,4,3200]{2,1,0:T(4,128)} reshape(f32[3,12800]{1,0:T(4,128)} %fusion.10) | data formatting | bytes 307200 | tf_op jit(solution)/shard_map/reshape | solution.py:86
  53.4 1.6 stack.9
  55.0 1.6 stack.10
  56.5 1.6 maximum_bitcast_fusion
  58.2 4.3 %all-to-all-start.3 = ((f32[32,2,400]{2,1,0:T(2,128)}), f32[32,2,400]{2,1,0:T(2,128)}, u32[]{:S(2)}, u32[]{:S(2)}) async-start(f32[32,2,400]{2,1,0:T(2,128)} %maximum_bitcast_fusion), calls=%async_computation.3 | async-start | bytes 262144 | tf_op jit(solution)/shard_map/all_to_all | solution.py:32
  62.5 0.9 multiply_convert_fusion
  63.5 15.1 %all_gather.12 = bf16[3,16,3200]{2,0,1:T(4,128)(2,1)S(1)} all-gather(bf16[3,4,3200]{2,0,1:T(4,128)(2,1)S(1)} %copy.35), channel_id=1, replica_groups=mesh['node'=8,'local'=4] {'local'}, dimensions={1}, use_global_device_ids=true | all-gather | bytes 384000 | tf_op jit(solution)/shard_map/all_gather | solution.py:89
  78.6 0.8 copy.36
  79.3 2.6 %reshape_reshape.3 = bf16[48,8,400]{2,1,0:T(8,128)(2,1)} reshape(bf16[3,16,3200]{2,1,0:T(8,128)(2,1)} %copy.36) | data formatting | bytes 614400 | tf_op jit(solution)/shard_map/reshape;reshape | solution.py:98
  81.9 1.9 %copy.38 = bf16[48,8,400]{2,0,1:T(8,128)(2,1)} copy(bf16[48,8,400]{2,1,0:T(8,128)(2,1)} %reshape_reshape.3) | data formatting | bytes 614400 | tf_op jit(solution)/shard_map/reshape;reshape | solution.py:98
  83.8 0.0 all-to-all-done.3
  83.8 4.1 %all-to-all-start.2 = ((bf16[48,8,400]{2,0,1:T(8,128)(2,1)}), bf16[48,8,400]{2,0,1:T(8,128)(2,1)}, u32[]{:S(2)}, u32[]{:S(2)}) async-start(bf16[48,8,400]{2,0,1:T(8,128)(2,1)} %copy.38), calls=%async_computation.2 | async-start | bytes 786432 | tf_op jit(solution)/shard_map/all_to_all | solution.py:99
  87.9 0.0 copy-done
  87.9 0.0 copy-done.2
  87.9 2.7 %fusion.1 = bf16[48,536]{1,0:T(8,128)(2,1)} fusion(bf16[48,3200]{1,0:T(8,128)(2,1)} %bitcast.59, bf16[3200,536]{0,1:T(8,128)(2,1)S(1)} %copy-done, f32[48,536]{1,0:T(8,128)S(1)} %copy-done.2, bf16[48,536]{1,0:T(8,128)(2,1)} %bitcast.61), kind=kOutput, calls=%fused_computation.3 | convolution fusion | flops 164865024 | bytes 3943424 | tf_op jit(solution)/shard_map/dot_general | solution.py:96
  90.7 1.0 reduce_sum.99
  91.6 70.0 %all-gather.1 = f32[32,2,400]{2,1,0:T(2,128)S(1)} all-gather(f32[1,2,400]{2,1,0:T(2,128)S(1)} %bitcast.63), channel_id=2, replica_groups=mesh['node'=8,'local'=4] {'node','local'}, dimensions={0}, use_global_device_ids=true | all-gather | bytes 105600 | tf_op jit(solution)/shard_map/all_gather | solution.py:34
  161.6 0.7 copy.39
  162.3 1.7 %reshape.82 = f32[2,12800]{1,0:T(2,128)} reshape(f32[2,32,400]{2,1,0:T(8,128)} %copy.39) | data formatting | bytes 204800 | tf_op jit(solution)/shard_map/reshape | solution.py:35
  164.1 0.0 all-to-all-done.2
  164.1 2.6 %fusion.27 = f32[400,536]{1,0:T(8,128)} fusion(bf16[384,400]{1,0:T(8,128)(2,1)} %bitcast.11, bf16[384,536]{1,0:T(8,128)(2,1)} %all_gather.13), kind=kOutput, calls=%fused_computation.51 | convolution fusion | flops 164659200 | bytes 1576448 | tf_op jit(solution)/shard_map/dot_general | solution.py:102
  (5 shorter events, 0.1 us)
Async XLA Ops:
  0.6 87.3 %copy-start = (bf16[3200,536]{0,1:T(8,128)(2,1)S(1)}, bf16[3200,536]{0,1:T(8,128)(2,1)}, u32[]{:S(2)}) copy-start(bf16[3200,536]{0,1:T(8,128)(2,1)} %param.14) | copy-start | bytes 10291204
  0.6 47.2 %copy-start.1 = (bf16[3,1,12800]{2,0,1:T(4,128)(2,1)S(1)}, bf16[3,1,12800]{2,0,1:T(4,128)(2,1)}, u32[]{:S(2)}) copy-start(bf16[3,1,12800]{2,0,1:T(4,128)(2,1)} %param.11) | copy-start | bytes 230404
  4.3 23.0 %all-to-all-start = ((bf16[2,4,12800]{2,0,1:T(2,128)(2,1)}), bf16[2,4,12800]{2,0,1:T(2,128)(2,1)}, u32[]{:S(2)}, u32[]{:S(2)}) async-start(bf16[2,4,12800]{2,0,1:T(2,128)(2,1)} %copy.33), calls=%async_computation | async-start | bytes 409600 | tf_op jit(solution)/shard_map/all_to_all | solution.py:53
  35.3 10.4 %all-to-all-start.1 = ((bf16[8,2,6400]{2,1,0:T(2,128)(2,1)}), bf16[8,2,6400]{2,1,0:T(2,128)(2,1)}, u32[]{:S(2)}, u32[]{:S(2)}) async-start(bf16[8,2,6400]{2,1,0:T(2,128)(2,1)} %reshape.88), calls=%async_computation.1 | async-start | bytes 409600 | tf_op jit(solution)/shard_map/all_to_all | solution.py:68
  51.6 36.3 %copy-start.2 = (f32[48,536]{1,0:T(8,128)S(1)}, f32[48,536]{1,0:T(8,128)}, u32[]{:S(2)}) copy-start(f32[48,536]{1,0:T(8,128)} %get-tuple-element.10) | copy-start | bytes 308740
  58.2 25.6 %all-to-all-start.3 = ((f32[32,2,400]{2,1,0:T(2,128)}), f32[32,2,400]{2,1,0:T(2,128)}, u32[]{:S(2)}, u32[]{:S(2)}) async-start(f32[32,2,400]{2,1,0:T(2,128)} %maximum_bitcast_fusion), calls=%async_computation.3 | async-start | bytes 262144 | tf_op jit(solution)/shard_map/all_to_all | solution.py:32
  83.8 80.3 %all-to-all-start.2 = ((bf16[48,8,400]{2,0,1:T(8,128)(2,1)}), bf16[48,8,400]{2,0,1:T(8,128)(2,1)}, u32[]{:S(2)}, u32[]{:S(2)}) async-start(bf16[48,8,400]{2,0,1:T(8,128)(2,1)} %copy.38), calls=%async_computation.2 | async-start | bytes 786432 | tf_op jit(solution)/shard_map/all_to_all | solution.py:99

commit v2 on v0

v2 whole, which is shorter than its diff:
```python
import functools
import jax
import jax.numpy as jnp
from jax import lax
from jax.experimental import pallas as pl
from jax.experimental.pallas import tpu as pltpu
from jax.sharding import PartitionSpec as P

epsilon = 1e-06
half_root = 0.7071067811865476
inv_root_two_pi = 0.3989422804014327
MESH = pl.DeviceIdType.MESH


def gelu_parts(preact):
    normal_cdf = 0.5 * (1.0 + lax.erf(preact * half_root))
    density = jnp.exp(-0.5 * preact * preact) * inv_root_two_pi
    return (preact * normal_cdf, normal_cdf + preact * density)


def each(count, step):
    if count <= 8:
        for k in range(1, count):
            step(k)
    else:
        lax.fori_loop(1, count, lambda k, none: (step(k), none)[1], 0)


class Exchange:
    def __init__(self, axis, count, source, land, send_sem, recv_sem):
        self.axis, self.count, self.source, self.land = axis, count, source, land
        self.send_sem, self.recv_sem = send_sem, recv_sem
        self.me = lax.axis_index(axis)

    def copy(self, k):
        peer = lax.rem(self.me + k, self.count)
        return pltpu.make_async_remote_copy(
            src_ref=self.source(peer),
            dst_ref=self.land.at[self.me],
            send_sem=self.send_sem.at[k],
            recv_sem=self.recv_sem.at[k],
            device_id={self.axis: peer},
            device_id_type=MESH,
        )

    def start(self):
        each(self.count, lambda k: self.copy(k).start())

    def wait_recv(self):
        def one(k):
            origin = lax.rem(self.me + self.count - k, self.count)
            pltpu.make_async_remote_copy(
                src_ref=self.source(origin),
                dst_ref=self.land.at[origin],
                send_sem=self.send_sem.at[k],
                recv_sem=self.recv_sem.at[k],
                device_id={self.axis: origin},
                device_id_type=MESH,
            ).wait_recv()

        each(self.count, one)

    def wait_send(self):
        each(self.count, lambda k: self.copy(k).wait_send())


def kernel(
    sizes,
    up_ref, block_ref, owner_ref, vis_ref, gain_ref, scale_ref, weight_hbm, pre_ref,
    hid_ref, down_ref, norm_ref,
    slot_tab, up_f, send_a, land_a, send_b, land_b, normed_f, gain_f, grad_f,
    land_c, rows_x, land_d, land_act, pre_f, deriv_f, hid_f, acc_f, terms_f, norm_s, land_n1, sum_n, land_n2, land_n3,
    weight_v, weight_sem, sems_l, sems_n,
):
    nodes, locs, caps, merge, here, width, model, units, images, share, window, group = sizes
    node, loc = lax.axis_index("node"), lax.axis_index("local")
    blocks = locs * here
    row_count = locs * caps * merge
    columns = model // nodes
    f32, bf16 = jnp.float32, jnp.bfloat16

    weight_copy = pltpu.make_async_copy(weight_hbm, weight_v, weight_sem)
    weight_copy.start()

    barrier = pltpu.get_barrier_semaphore()

    def greet(axis, count, me):
        def one(k):
            pl.semaphore_signal(
                barrier, inc=1, device_id={axis: lax.rem(me + k, count)}, device_id_type=MESH
            )

        each(count, one)

    greet("local", locs, loc)
    greet("node", nodes, node)

    for b in range(here):
        for q in range(merge):
            part = up_ref[b * locs : (b + 1) * locs, q * model : (q + 1) * model].astype(f32)
            up_f[:, b * merge + q, :] = part
    send_a[...] = up_f[...].astype(bf16)
    land_a[pl.ds(loc, 1)] = send_a[pl.ds(loc, 1)]

    pl.semaphore_wait(barrier, locs + nodes - 2)
    move_a = Exchange("local", locs, lambda p: send_a.at[p], land_a, sems_l.at[0], sems_l.at[1])
    move_a.start()

    for t in range(locs):
        for s in range(caps):
            at = (t * caps + s) * merge
            pre_f[at : at + merge, :] = pre_ref[s, t * merge : (t + 1) * merge, :].astype(f32)
    activation, derivative = gelu_parts(pre_f[...])
    deriv_f[...] = derivative
    land_act[pl.ds(node, 1)] = activation.astype(bf16)[None]
    move_act = Exchange("node", nodes, lambda p: land_act.at[node], land_act, sems_n.at[0], sems_n.at[1])
    move_act.start()

    for q in range(merge):
        normed_f[:, q, :] = vis_ref[:, q * model : (q + 1) * model].astype(f32)
        gain_f[q : q + 1, :] = gain_ref[:, q * model : (q + 1) * model]
    count_in = 1.0 / width

    def mean(x):
        return jnp.sum(jnp.sum(x, axis=2, keepdims=True), axis=1, keepdims=True) * count_in

    inputs = normed_f[...]
    centred = inputs - mean(inputs)
    inv_std = lax.rsqrt(mean(centred * centred) + epsilon)
    normed_f[...] = centred * inv_std

    t_shape = (nodes * merge, blocks * merge)
    t_row = lax.broadcasted_iota(jnp.int32, t_shape, 0)
    t_col = lax.broadcasted_iota(jnp.int32, t_shape, 1)
    col_block = t_col // merge
    col_owner = jnp.full(t_shape, -1, jnp.int32)
    for b in range(blocks):
        owner = owner_ref[block_ref[node * blocks + b]]
        col_owner = jnp.where(col_block == b, owner, col_owner)
    to_owner = jnp.where(
        (t_row // merge == col_owner) & (t_row % merge == t_col % merge), 1.0, 0.0
    ).astype(bf16)

    taken = jnp.int32(0)
    for j in range(images):
        mine = owner_ref[j] == node
        slot_tab[j] = jnp.where(mine, taken, -1)
        taken = taken + jnp.where(mine, 1, 0)
    p_shape = (caps * merge, nodes * merge)
    p_row = lax.broadcasted_iota(jnp.int32, p_shape, 0)
    p_col = lax.broadcasted_iota(jnp.int32, p_shape, 1)
    col_node = p_col // merge

    def source(n, col_slot):
        slot = jnp.int32(-1)
        for b in range(blocks):
            slot = jnp.maximum(slot, slot_tab[block_ref[n * blocks + b]])
        return jnp.where(col_node == n, slot, col_slot)

    col_slot = jnp.full(p_shape, -1, jnp.int32)
    if nodes <= 8:
        for n in range(nodes):
            col_slot = source(n, col_slot)
    else:
        col_slot = lax.fori_loop(0, nodes, source, col_slot)
    pick = jnp.where(
        (p_row // merge == col_slot) & (p_row % merge == p_col % merge), 1.0, 0.0
    ).astype(bf16)

    move_a.wait_recv()
    arrived = land_a[...].astype(f32).reshape(blocks * merge, model).astype(bf16)
    sums = jnp.dot(to_owner, arrived, preferred_element_type=f32)
    send_b[...] = sums.reshape(nodes, merge, model).astype(bf16)
    move_b = Exchange("node", nodes, lambda p: send_b.at[p], land_b, sems_n.at[2], sems_n.at[3])
    move_b.start()
    land_b[pl.ds(node, 1)] = send_b[pl.ds(node, 1)]
    move_b.wait_recv()
    from_nodes = land_b[...].astype(f32).reshape(nodes * merge, model).astype(bf16)
    grad_f[...] = jnp.dot(pick, from_nodes, preferred_element_type=f32).reshape(caps, merge, model)

    grads = grad_f[...]
    normed = normed_f[...]
    scaled = grads * gain_f[...][None]
    input_grad = inv_std * (scaled - mean(scaled) - normed * mean(scaled * normed))
    branch = input_grad * scale_ref[...][None]
    land_c[pl.ds(loc, 1)] = branch.astype(bf16)[None]
    move_c = Exchange("local", locs, lambda p: land_c.at[loc], land_c, sems_l.at[2], sems_l.at[3])
    move_c.start()

    if share * locs > width:
        terms_f[:, width:] = jnp.zeros((2, share * locs - width), f32)
    gain_terms = jnp.sum(grads * normed, axis=0)
    bias_terms = jnp.sum(grads, axis=0)
    for q in range(merge):
        terms_f[0:1, q * model : (q + 1) * model] = gain_terms[q : q + 1, :]
        terms_f[1:2, q * model : (q + 1) * model] = bias_terms[q : q + 1, :]
    for t in range(locs):
        norm_s[t] = terms_f[:, t * share : (t + 1) * share]
    land_n1[pl.ds(loc, 1)] = norm_s[pl.ds(loc, 1)]
    move_n1 = Exchange("local", locs, lambda p: norm_s.at[p], land_n1, sems_l.at[4], sems_l.at[5])
    move_n1.start()

    move_c.wait_recv()
    rows_x[...] = land_c[...].astype(f32).reshape(row_count, model).astype(bf16)

    def window_at(n):
        low = jnp.minimum((n * columns) // 128, (model - window) // 128)
        return pl.multiple_of(low * 128, 128)

    move_d = Exchange(
        "node", nodes, lambda p: rows_x.at[:, pl.ds(window_at(p), window)], land_d, sems_n.at[4], sems_n.at[5]
    )
    move_d.start()
    land_d[pl.ds(node, 1)] = rows_x[:, pl.ds(window_at(node), window)][None]

    move_n1.wait_recv()
    sum_n[...] = jnp.sum(land_n1[...], axis=0)
    land_n2[pl.ds(node, 1)] = sum_n[...][None]
    move_n2 = Exchange("node", nodes, lambda p: sum_n, land_n2, sems_n.at[6], sems_n.at[7])
    move_n2.start()

    weight_copy.wait()
    hidden_in = lax.dot_general(
        rows_x[...], weight_v[...], (((1,), (1,)), ((), ())), preferred_element_type=f32
    )
    pre_f[...] = hidden_in * deriv_f[...]
    for t in range(locs):
        for s in range(caps):
            at = (t * caps + s) * merge
            hid_f[s, t * merge : (t + 1) * merge, :] = pre_f[at : at + merge, :]
    hid_ref[...] = hid_f[...].astype(bf16)

    move_n2.wait_recv()
    land_n3[pl.ds(loc, 1)] = jnp.sum(land_n2[...], axis=0)[None]
    move_n3 = Exchange("local", locs, lambda p: land_n3.at[loc], land_n3, sems_l.at[6], sems_l.at[7])
    move_n3.start()

    move_d.wait_recv()
    move_act.wait_recv()

    def product(first):
        left = land_d[pl.ds(first, group)].reshape(group * row_count, window)
        right = land_act[pl.ds(first, group)].reshape(group * row_count, units)
        return lax.dot_general(left, right, (((0,), (0,)), ((), ())), preferred_element_type=f32)

    acc_f[...] = product(0)
    if nodes > group:

        def more(g, none):
            acc_f[...] += product(g * group)
            return none

        lax.fori_loop(1, nodes // group, more, 0)
    skip = node * columns - window_at(node)
    if columns % 8 == 0:
        down_ref[...] = acc_f[pl.ds(pl.multiple_of(skip, 8), columns), :]
    else:
        down_ref[...] = pltpu.roll(acc_f[...], lax.rem(window - skip, window), 0)[:columns, :]

    move_n3.wait_recv()
    for t in range(locs):
        low, high = t * share, min((t + 1) * share, width)
        if high > low:
            norm_ref[:, low:high] = land_n3[t, :, : high - low]

    for move in (move_a, move_act, move_b, move_c, move_n1, move_d, move_n2, move_n3):
        move.wait_send()


def body(
    upstream, block_image, image_owner, vision_out, norm_gain, layer_scale, down_weight, hidden_pre
):
    locs = lax.axis_size("local")
    nodes = lax.axis_size("node")
    width = upstream.shape[1]
    model = layer_scale.shape[0]
    merge = width // model
    here = upstream.shape[0] // locs
    images = image_owner.shape[0]
    caps = vision_out.shape[0]
    units = down_weight.shape[1]
    columns = model // nodes
    row_count = locs * caps * merge
    share = -(-width // (locs * 128)) * 128
    window = max(
        -(-(n * columns + columns) // 128) * 128 - (n * columns) // 128 * 128 for n in range(nodes)
    )
    group = max(g for g in range(1, nodes + 1) if nodes % g == 0 and (g == 1 or g * row_count <= 512))
    sizes = (nodes, locs, caps, merge, here, width, model, units, images, share, window, group)
    f32, bf16 = jnp.float32, jnp.bfloat16
    vmem = pl.BlockSpec(memory_space=pltpu.VMEM)
    smem = pl.BlockSpec(memory_space=pltpu.SMEM)
    return pl.pallas_call(
        functools.partial(kernel, sizes),
        out_shape=(
            jax.ShapeDtypeStruct(hidden_pre.shape, bf16),
            jax.ShapeDtypeStruct((columns, units), f32),
            jax.ShapeDtypeStruct((2, width), f32),
        ),
        in_specs=[vmem, smem, smem, vmem, vmem, vmem, pl.BlockSpec(memory_space=pl.ANY), vmem],
        out_specs=(vmem, vmem, vmem),
        scratch_shapes=[
            pltpu.SMEM((images,), jnp.int32),
            pltpu.VMEM((locs, here * merge, model), f32),
            pltpu.VMEM((locs, here * merge, model), bf16),
            pltpu.VMEM((locs, here * merge, model), bf16),
            pltpu.VMEM((nodes, merge, model), bf16),
            pltpu.VMEM((nodes, merge, model), bf16),
            pltpu.VMEM((caps, merge, model), f32),
            pltpu.VMEM((merge, model), f32),
            pltpu.VMEM((caps, merge, model), f32),
            pltpu.VMEM((locs, caps, merge, model), bf16),
            pltpu.VMEM((row_count, model), bf16),
            pltpu.VMEM((nodes, row_count, window), bf16),
            pltpu.VMEM((nodes, row_count, units), bf16),
            pltpu.VMEM((row_count, units), f32),
            pltpu.VMEM((row_count, units), f32),
            pltpu.VMEM((caps, locs * merge, units), f32),
            pltpu.VMEM((window, units), f32),
            pltpu.VMEM((2, locs * share), f32),
            pltpu.VMEM((locs, 2, share), f32),
            pltpu.VMEM((locs, 2, share), f32),
            pltpu.VMEM((2, share), f32),
            pltpu.VMEM((nodes, 2, share), f32),
            pltpu.VMEM((locs, 2, share), f32),
            pltpu.VMEM((units, model), bf16),
            pltpu.SemaphoreType.DMA,
            pltpu.SemaphoreType.DMA((8, locs)),
            pltpu.SemaphoreType.DMA((8, nodes)),
        ],
        compiler_params=pltpu.CompilerParams(
            collective_id=0, has_side_effects=True, vmem_limit_bytes=56 * 1024 * 1024
        ),
    )(
        upstream,
        block_image,
        image_owner,
        vision_out.reshape(caps, width),
        norm_gain.reshape(1, width),
        layer_scale.reshape(1, model),
        down_weight.T,
        hidden_pre,
    )


def solution(mesh):
    placed = (
        P(("node", "local"), None),
        P(),
        P(),
        P("node", "local", None),
        P(),
        P(),
        P(None, "local"),
        P("node", None, "local"),
    )
    return jax.shard_map(
        body,
        mesh=mesh,
        in_specs=placed,
        out_specs=(P("node", None, "local"), P("node", "local"), P()),
        check_vma=False,
    )
```

time: 195 us -> 49.7 us (0.25)
  waiting for transfers between devices: 96.7 us -> 0 us
  Pallas kernels: 0 us -> 40.7 us
  blocking collectives: 26.2 us -> 0 us
  starting transfers between devices: 14.5 us -> 0 us
  between operations: 14.1 us -> 0.64 us
  local copies, waits for them, and re-layouts: 20.6 us -> 8.03 us
  other arithmetic: 12.1 us -> 0 us
  matrix products: 9.27 us -> 0 us
    psum x1 -> x0, waiting for transfers between devices: 84.8 us -> none  [flat_norms(): return lax.psum(norm_terms, ('node', 'local'))]
    pallas_call x0 -> x1, Pallas kernels: none -> 40.7 us  [body(): pl.pallas_call(functools.partial(kernel, sizes), out_shape=(jax.ShapeDtyp...]
    all_gather x2 -> x0, blocking collectives: 26.2 us -> none  [the longest x1 15.3 us: body(): patches = lax.all_gather(branch, 'local', axis=1, tiled=True)]
    all_to_all x3 -> x0, starting transfers between devices: 14.4 us -> none  [the longest x1 6.32 us: body(): lax.all_to_all(by_block, 'local', split_axis=1, concat_axis=0, tiled=True)]
    all_to_all x3 -> x0, waiting for transfers between devices: 11.9 us -> none  [the longest x1 6.27 us: body(): lax.all_to_all(node_sums, 'node', split_axis=0, concat_axis=0, tiled=True)]
    dot_general x4 -> x0, matrix products: 9.27 us -> none  [the longest x1 2.74 us: body(): jnp.dot(patch_rows, down_weight, preferred_element_type=jnp.float32)]
    another operation x4 -> x0, local copies, waits for them, and re-layouts: 5.94 us -> none  [the longest x2 4.45 us: body(): by_column = patch_rows.reshape(row_count, node_count, shard_rows)]
    reshape x6 -> x2, local copies, waits for them, and re-layouts: 7.18 us -> 2.79 us  [the longest x1 1.46 us: body(): norm_gain.reshape(1, width)]
  transfers between devices with their start and end apart: 4 -> 0, of which waited for: 3 -> 0; matrix products, arithmetic and copies ran while one was open for 8% -> 0% of each run, Pallas kernels for 0% -> 0%
where the time goes in v2:
time: 49.7 us; the launch traced here: 49.3 us
  Pallas kernels  40.7 us (82%)
  local copies, waits for them, and re-layouts  8.03 us (16%)
  between operations  0.64 us (1%)
    pallas_call x1, Pallas kernels, body(): pl.pallas_call(functools.partial(kernel, sizes), out_shape=(jax.ShapeDtyp...  40.7 us
    unnamed x3, local copies, waits for them, and re-layouts  5.24 us
    reshape x1, local copies, waits for them, and re-layouts, body(): norm_gain.reshape(1, width)  1.46 us
    reshape x1, local copies, waits for them, and re-layouts, body(): layer_scale.reshape(1, model)  1.33 us

profile of v2, /device:TPU:0, one launch (start us, length us, event | category | flops | bytes accessed | tf_op | source)
XLA Modules:
  0.0 49.3 jit_solution(10498928188269162481)
XLA Ops:
  0.6 1.3 %reshape.17.scale_ref = f32[1,3200]{1,0:T(1,128)} reshape(f32[3200]{0:T(1024)} %param.13) | data formatting | bytes 25600 | tf_op jit(solution)/shard_map/reshape | solution.py:340
  2.0 1.5 %reshape.16.gain_ref = f32[1,12800]{1,0:T(1,128)} reshape(f32[12800]{0:T(1024)} %param.12) | data formatting | bytes 102400 | tf_op jit(solution)/shard_map/reshape | solution.py:339
  3.4 40.7 %shard_map.103 = (bf16[3,16,536]{2,1,0:T(8,128)(2,1)}, f32[400,536]{1,0:T(8,128)}, f32[2,12800]{1,0:T(2,128)}) custom-call(bf16[8,12800]{1,0:T(8,128)(2,1)} %up_ref.1, s32[64]{0:T(128)} %block_ref.1, s32[16]{0:T(128)} %owner_ref.1, bf16[3,12800]{1,0:T(4,128)(2,1)} %bitcast.3, f32[1,12800]{1,0:T(1,128)} %reshape.16.gain_ref, f32[1,3200]{1,0:T(1,128)} %reshape.17.scale_ref, ...), custom_call_target="tpu_custom_call" | custom-call | tf_op jit(solution)/shard_map/pallas_call | solution.py:293
  44.1 1.5 %copy.14 = bf16[3,16,536]{2,1,0:T(8,128)(2,1)} copy(bf16[3,16,536]{2,1,0:T(8,128)(2,1)} %get-tuple-element.6) | data formatting | bytes 102912
  45.5 2.2 %copy.15 = f32[400,536]{1,0:T(8,128)} copy(f32[400,536]{1,0:T(8,128)} %get-tuple-element.7) | data formatting | bytes 1715200
  47.8 1.5 %copy.16 = f32[2,12800]{1,0:T(2,128)} copy(f32[2,12800]{1,0:T(2,128)} %get-tuple-element.8) | data formatting | bytes 204800

commit v3 on v2

--- a/solution.py
+++ b/solution.py
@@ -66,11 +66,11 @@
 
 def kernel(
     sizes,
-    up_ref, block_ref, owner_ref, vis_ref, gain_ref, scale_ref, weight_hbm, pre_ref,
+    up_ref, block_ref, owner_ref, vis_ref, gain_hbm, scale_hbm, weight_hbm, pre_ref,
     hid_ref, down_ref, norm_ref,
     slot_tab, up_f, send_a, land_a, send_b, land_b, normed_f, gain_f, grad_f,
-    land_c, rows_x, land_d, land_act, pre_f, deriv_f, hid_f, acc_f, terms_f, norm_s, land_n1, sum_n, land_n2, land_n3,
-    weight_v, weight_sem, sems_l, sems_n,
+    land_c, rows_x, land_d, land_act, pre_f, deriv_f, hid_f, acc_f, terms_f, norm_s, land_n1, land_n2, land_n3,
+    weight_v, scale_v, own_sems, sems_l, sems_n,
 ):
     nodes, locs, caps, merge, here, width, model, units, images, share, window, group = sizes
     node, loc = lax.axis_index("node"), lax.axis_index("local")
@@ -79,7 +79,16 @@
     columns = model // nodes
     f32, bf16 = jnp.float32, jnp.bfloat16
 
-    weight_copy = pltpu.make_async_copy(weight_hbm, weight_v, weight_sem)
+    weight_copy = pltpu.make_async_copy(weight_hbm, weight_v, own_sems.at[0])
+    param_copies = [pltpu.make_async_copy(scale_hbm, scale_v.at[0], own_sems.at[1])]
+    for q in range(merge):
+        param_copies.append(
+            pltpu.make_async_copy(
+                gain_hbm.at[pl.ds(q * model, model)], gain_f.at[q], own_sems.at[2 + q]
+            )
+        )
+    for copy in param_copies:
+        copy.start()
     weight_copy.start()
 
     barrier = pltpu.get_barrier_semaphore()
@@ -118,7 +127,6 @@
 
     for q in range(merge):
         normed_f[:, q, :] = vis_ref[:, q * model : (q + 1) * model].astype(f32)
-        gain_f[q : q + 1, :] = gain_ref[:, q * model : (q + 1) * model]
     count_in = 1.0 / width
 
     def mean(x):
@@ -178,27 +186,34 @@
     from_nodes = land_b[...].astype(f32).reshape(nodes * merge, model).astype(bf16)
     grad_f[...] = jnp.dot(pick, from_nodes, preferred_element_type=f32).reshape(caps, merge, model)
 
+    for copy in param_copies:
+        copy.wait()
     grads = grad_f[...]
     normed = normed_f[...]
     scaled = grads * gain_f[...][None]
     input_grad = inv_std * (scaled - mean(scaled) - normed * mean(scaled * normed))
-    branch = input_grad * scale_ref[...][None]
+    branch = input_grad * scale_v[...][None]
     land_c[pl.ds(loc, 1)] = branch.astype(bf16)[None]
     move_c = Exchange("local", locs, lambda p: land_c.at[loc], land_c, sems_l.at[2], sems_l.at[3])
     move_c.start()
 
-    if share * locs > width:
-        terms_f[:, width:] = jnp.zeros((2, share * locs - width), f32)
+    if share * nodes > width:
+        terms_f[:, width:] = jnp.zeros((2, share * nodes - width), f32)
     gain_terms = jnp.sum(grads * normed, axis=0)
     bias_terms = jnp.sum(grads, axis=0)
     for q in range(merge):
         terms_f[0:1, q * model : (q + 1) * model] = gain_terms[q : q + 1, :]
         terms_f[1:2, q * model : (q + 1) * model] = bias_terms[q : q + 1, :]
-    for t in range(locs):
-        norm_s[t] = terms_f[:, t * share : (t + 1) * share]
-    land_n1[pl.ds(loc, 1)] = norm_s[pl.ds(loc, 1)]
-    move_n1 = Exchange("local", locs, lambda p: norm_s.at[p], land_n1, sems_l.at[4], sems_l.at[5])
+    for n in range(nodes):
+        norm_s[n] = terms_f[:, n * share : (n + 1) * share]
+    move_n1 = Exchange("node", nodes, lambda p: norm_s.at[p], land_n1, sems_n.at[6], sems_n.at[7])
     move_n1.start()
+    land_n1[pl.ds(node, 1)] = norm_s[pl.ds(node, 1)]
+
+    move_n1.wait_recv()
+    land_n2[pl.ds(loc, 1)] = jnp.sum(land_n1[...], axis=0)[None]
+    move_n2 = Exchange("local", locs, lambda p: land_n2.at[loc], land_n2, sems_l.at[4], sems_l.at[5])
+    move_n2.start()
 
     move_c.wait_recv()
     rows_x[...] = land_c[...].astype(f32).reshape(row_count, model).astype(bf16)
@@ -213,11 +228,10 @@
     move_d.start()
     land_d[pl.ds(node, 1)] = rows_x[:, pl.ds(window_at(node), window)][None]
 
-    move_n1.wait_recv()
-    sum_n[...] = jnp.sum(land_n1[...], axis=0)
-    land_n2[pl.ds(node, 1)] = sum_n[...][None]
-    move_n2 = Exchange("node", nodes, lambda p: sum_n, land_n2, sems_n.at[6], sems_n.at[7])
-    move_n2.start()
+    move_n2.wait_recv()
+    land_n3[pl.ds(node, 1)] = jnp.sum(land_n2[...], axis=0)[None]
+    move_n3 = Exchange("node", nodes, lambda p: land_n3.at[node], land_n3, sems_n.at[8], sems_n.at[9])
+    move_n3.start()
 
     weight_copy.wait()
     hidden_in = lax.dot_general(
@@ -230,11 +244,6 @@
             hid_f[s, t * merge : (t + 1) * merge, :] = pre_f[at : at + merge, :]
     hid_ref[...] = hid_f[...].astype(bf16)
 
-    move_n2.wait_recv()
-    land_n3[pl.ds(loc, 1)] = jnp.sum(land_n2[...], axis=0)[None]
-    move_n3 = Exchange("local", locs, lambda p: land_n3.at[loc], land_n3, sems_l.at[6], sems_l.at[7])
-    move_n3.start()
-
     move_d.wait_recv()
     move_act.wait_recv()
 
@@ -258,13 +267,21 @@
         down_ref[...] = pltpu.roll(acc_f[...], lax.rem(window - skip, window), 0)[:columns, :]
 
     move_n3.wait_recv()
-    for t in range(locs):
-        low, high = t * share, min((t + 1) * share, width)
+    for n in range(nodes):
+        low, high = n * share, min((n + 1) * share, width)
         if high > low:
-            norm_ref[:, low:high] = land_n3[t, :, : high - low]
+            norm_ref[:, low:high] = land_n3[n, :, : high - low]
 
     for move in (move_a, move_act, move_b, move_c, move_n1, move_d, move_n2, move_n3):
         move.wait_send()
+
+
+def settle(*refs):
+    copies = [pltpu.make_async_copy(refs[i], refs[3 + i], refs[6].at[i]) for i in range(3)]
+    for copy in copies:
+        copy.start()
+    for copy in copies:
+        copy.wait()
 
 
 def body(
@@ -281,7 +298,7 @@
     units = down_weight.shape[1]
     columns = model // nodes
     row_count = locs * caps * merge
-    share = -(-width // (locs * 128)) * 128
+    share = -(-width // (nodes * 128)) * 128
     window = max(
         -(-(n * columns + columns) // 128) * 128 - (n * columns) // 128 * 128 for n in range(nodes)
     )
@@ -290,14 +307,16 @@
     f32, bf16 = jnp.float32, jnp.bfloat16
     vmem = pl.BlockSpec(memory_space=pltpu.VMEM)
     smem = pl.BlockSpec(memory_space=pltpu.SMEM)
-    return pl.pallas_call(
+    anywhere = pl.BlockSpec(memory_space=pl.ANY)
+    shapes = (
+        jax.ShapeDtypeStruct(hidden_pre.shape, bf16),
+        jax.ShapeDtypeStruct((columns, units), f32),
+        jax.ShapeDtypeStruct((2, width), f32),
+    )
+    results = pl.pallas_call(
         functools.partial(kernel, sizes),
-        out_shape=(
-            jax.ShapeDtypeStruct(hidden_pre.shape, bf16),
-            jax.ShapeDtypeStruct((columns, units), f32),
-            jax.ShapeDtypeStruct((2, width), f32),
-        ),
-        in_specs=[vmem, smem, smem, vmem, vmem, vmem, pl.BlockSpec(memory_space=pl.ANY), vmem],
+        out_shape=shapes,
+        in_specs=[vmem, smem, smem, vmem, anywhere, anywhere, anywhere, vmem],
         out_specs=(vmem, vmem, vmem),
         scratch_shapes=[
             pltpu.SMEM((images,), jnp.int32),
@@ -317,16 +336,16 @@
             pltpu.VMEM((row_count, units), f32),
             pltpu.VMEM((caps, locs * merge, units), f32),
             pltpu.VMEM((window, units), f32),
-            pltpu.VMEM((2, locs * share), f32),
-            pltpu.VMEM((locs, 2, share), f32),
-            pltpu.VMEM((locs, 2, share), f32),
-            pltpu.VMEM((2, share), f32),
+            pltpu.VMEM((2, nodes * share), f32),
+            pltpu.VMEM((nodes, 2, share), f32),
             pltpu.VMEM((nodes, 2, share), f32),
             pltpu.VMEM((locs, 2, share), f32),
+            pltpu.VMEM((nodes, 2, share), f32),
             pltpu.VMEM((units, model), bf16),
-            pltpu.SemaphoreType.DMA,
-            pltpu.SemaphoreType.DMA((8, locs)),
-            pltpu.SemaphoreType.DMA((8, nodes)),
+            pltpu.VMEM((1, model), f32),
+            pltpu.SemaphoreType.DMA((2 + merge,)),
+            pltpu.SemaphoreType.DMA((6, locs)),
+            pltpu.SemaphoreType.DMA((10, nodes)),
         ],
         compiler_params=pltpu.CompilerParams(
             collective_id=0, has_side_effects=True, vmem_limit_bytes=56 * 1024 * 1024
@@ -336,11 +355,19 @@
         block_image,
         image_owner,
         vision_out.reshape(caps, width),
-        norm_gain.reshape(1, width),
-        layer_scale.reshape(1, model),
+        norm_gain,
+        layer_scale,
         down_weight.T,
         hidden_pre,
     )
+    return pl.pallas_call(
+        settle,
+        out_shape=shapes,
+        in_specs=[anywhere] * 3,
+        out_specs=(vmem,) * 3,
+        scratch_shapes=[pltpu.SemaphoreType.DMA((3,))],
+        compiler_params=pltpu.CompilerParams(vmem_limit_bytes=56 * 1024 * 1024),
+    )(*results)
 
 
 def solution(mesh):

time: 49.7 us -> 36 us (0.72)
  local copies, waits for them, and re-layouts: 8.03 us -> 0 us
  Pallas kernels: 40.7 us -> 35.1 us
    pallas_call x1 -> x2, Pallas kernels: 40.7 us -> 35.1 us  [the longest x1 32.8 us: body(): pl.pallas_call(functools.partial(kernel, sizes), out_shape=shapes, in_spe...]
    unnamed x3 -> x0, local copies, waits for them, and re-layouts: 5.24 us -> none
    reshape x2 -> x0, local copies, waits for them, and re-layouts: 2.79 us -> none  [the longest x1 1.46 us: body(): norm_gain.reshape(1, width)]
where the time goes in v3:
time: 36 us; the launch traced here: 35.7 us
  Pallas kernels  35.1 us (98%)
  between operations  0.64 us (2%)
    pallas_call x1, Pallas kernels, body(): pl.pallas_call(functools.partial(kernel, sizes), out_shape=shapes, in_spe...  32.8 us
    pallas_call x1, Pallas kernels, body(): pl.pallas_call(settle, out_shape=shapes, in_specs=[anywhere] * 3, out_spe...  2.28 us

profile of v3, /device:TPU:0, one launch (start us, length us, event | category | flops | bytes accessed | tf_op | source)
XLA Modules:
  0.0 35.7 jit_solution(5211119284254021914)
XLA Ops:
  0.6 32.8 %shard_map.103 = (bf16[3,16,536]{2,1,0:T(8,128)(2,1)}, f32[400,536]{1,0:T(8,128)}, f32[2,12800]{1,0:T(2,128)}) custom-call(bf16[8,12800]{1,0:T(8,128)(2,1)} %up_ref.1, s32[64]{0:T(128)} %block_ref.1, s32[16]{0:T(128)} %owner_ref.1, bf16[3,12800]{1,0:T(4,128)(2,1)} %bitcast.3, f32[12800]{0:T(1024)} %gain_hbm.1, f32[3200]{0:T(1024)} %scale_hbm.1, ...), custom_call_target="tpu_custom_call" | custom-call | tf_op jit(solution)/shard_map/pallas_call | solution.py:316
  33.4 2.3 %shard_map.104 = (bf16[3,16,536]{2,1,0:T(8,128)(2,1)}, f32[400,536]{1,0:T(8,128)}, f32[2,12800]{1,0:T(2,128)}) custom-call(bf16[3,16,536]{2,1,0:T(8,128)(2,1)} %get-tuple-element.6.refs_0_, f32[400,536]{1,0:T(8,128)} %get-tuple-element.7.refs_1_, f32[2,12800]{1,0:T(2,128)} %get-tuple-element.8.refs_2_), custom_call_target="tpu_custom_call" | custom-call | tf_op jit(solution)/shard_map/pallas_call | solution.py:363

commit v4 on v3

--- a/solution.py
+++ b/solution.py
@@ -28,7 +28,8 @@
 
 class Exchange:
     def __init__(self, axis, count, source, land, send_sem, recv_sem):
-        self.axis, self.count, self.source, self.land = axis, count, source, land
+        self.axis, self.count, self.source = axis, count, source
+        self.land = land if callable(land) else lambda slot: land.at[slot]
         self.send_sem, self.recv_sem = send_sem, recv_sem
         self.me = lax.axis_index(axis)
 
@@ -36,7 +37,7 @@
         peer = lax.rem(self.me + k, self.count)
         return pltpu.make_async_remote_copy(
             src_ref=self.source(peer),
-            dst_ref=self.land.at[self.me],
+            dst_ref=self.land(self.me),
             send_sem=self.send_sem.at[k],
             recv_sem=self.recv_sem.at[k],
             device_id={self.axis: peer},
@@ -51,7 +52,7 @@
             origin = lax.rem(self.me + self.count - k, self.count)
             pltpu.make_async_remote_copy(
                 src_ref=self.source(origin),
-                dst_ref=self.land.at[origin],
+                dst_ref=self.land(origin),
                 send_sem=self.send_sem.at[k],
                 recv_sem=self.recv_sem.at[k],
                 device_id={self.axis: origin},
@@ -66,18 +67,31 @@
 
 def kernel(
     sizes,
-    up_ref, block_ref, owner_ref, vis_ref, gain_hbm, scale_hbm, weight_hbm, pre_ref,
+    up_hbm, block_ref, owner_ref, vis_hbm, gain_hbm, scale_hbm, weight_hbm, pre_hbm,
     hid_ref, down_ref, norm_ref,
     slot_tab, up_f, send_a, land_a, send_b, land_b, normed_f, gain_f, grad_f,
     land_c, rows_x, land_d, land_act, pre_f, deriv_f, hid_f, acc_f, terms_f, norm_s, land_n1, land_n2, land_n3,
-    weight_v, scale_v, own_sems, sems_l, sems_n,
+    weight_v, scale_v, up_ref, vis_ref, pre_ref, own_sems, sems_l, sems_n,
 ):
-    nodes, locs, caps, merge, here, width, model, units, images, share, window, group = sizes
+    nodes, locs, caps, merge, here, width, model, units, images, share, window, group, cut, early = sizes
     node, loc = lax.axis_index("node"), lax.axis_index("local")
     blocks = locs * here
     row_count = locs * caps * merge
     columns = model // nodes
     f32, bf16 = jnp.float32, jnp.bfloat16
+
+    barrier = pltpu.get_barrier_semaphore()
+
+    def greet(axis, count, me):
+        def one(k):
+            pl.semaphore_signal(
+                barrier, inc=1, device_id={axis: lax.rem(me + k, count)}, device_id_type=MESH
+            )
+
+        each(count, one)
+
+    greet("local", locs, loc)
+    greet("node", nodes, node)
 
     weight_copy = pltpu.make_async_copy(weight_hbm, weight_v, own_sems.at[0])
     param_copies = [pltpu.make_async_copy(scale_hbm, scale_v.at[0], own_sems.at[1])]
@@ -87,22 +101,16 @@
                 gain_hbm.at[pl.ds(q * model, model)], gain_f.at[q], own_sems.at[2 + q]
             )
         )
+    up_copy = pltpu.make_async_copy(up_hbm, up_ref, own_sems.at[2 + merge])
+    pre_copy = pltpu.make_async_copy(pre_hbm, pre_ref, own_sems.at[3 + merge])
+    vis_copy = pltpu.make_async_copy(vis_hbm, vis_ref, own_sems.at[4 + merge])
+    up_copy.start()
+    pre_copy.start()
+    vis_copy.start()
     for copy in param_copies:
         copy.start()
     weight_copy.start()
-
-    barrier = pltpu.get_barrier_semaphore()
-
-    def greet(axis, count, me):
-        def one(k):
-            pl.semaphore_signal(
-                barrier, inc=1, device_id={axis: lax.rem(me + k, count)}, device_id_type=MESH
-            )
-
-        each(count, one)
-
-    greet("local", locs, loc)
-    greet("node", nodes, node)
+    up_copy.wait()
 
     for b in range(here):
         for q in range(merge):
@@ -115,6 +123,7 @@
     move_a = Exchange("local", locs, lambda p: send_a.at[p], land_a, sems_l.at[0], sems_l.at[1])
     move_a.start()
 
+    pre_copy.wait()
     for t in range(locs):
         for s in range(caps):
             at = (t * caps + s) * merge
@@ -125,6 +134,7 @@
     move_act = Exchange("node", nodes, lambda p: land_act.at[node], land_act, sems_n.at[0], sems_n.at[1])
     move_act.start()
 
+    vis_copy.wait()
     for q in range(merge):
         normed_f[:, q, :] = vis_ref[:, q * model : (q + 1) * model].astype(f32)
     count_in = 1.0 / width
@@ -186,17 +196,8 @@
     from_nodes = land_b[...].astype(f32).reshape(nodes * merge, model).astype(bf16)
     grad_f[...] = jnp.dot(pick, from_nodes, preferred_element_type=f32).reshape(caps, merge, model)
 
-    for copy in param_copies:
-        copy.wait()
     grads = grad_f[...]
     normed = normed_f[...]
-    scaled = grads * gain_f[...][None]
-    input_grad = inv_std * (scaled - mean(scaled) - normed * mean(scaled * normed))
-    branch = input_grad * scale_v[...][None]
-    land_c[pl.ds(loc, 1)] = branch.astype(bf16)[None]
-    move_c = Exchange("local", locs, lambda p: land_c.at[loc], land_c, sems_l.at[2], sems_l.at[3])
-    move_c.start()
-
     if share * nodes > width:
         terms_f[:, width:] = jnp.zeros((2, share * nodes - width), f32)
     gain_terms = jnp.sum(grads * normed, axis=0)
@@ -210,28 +211,70 @@
     move_n1.start()
     land_n1[pl.ds(node, 1)] = norm_s[pl.ds(node, 1)]
 
+    for copy in param_copies:
+        copy.wait()
+    scaled = grads * gain_f[...][None]
+    input_grad = inv_std * (scaled - mean(scaled) - normed * mean(scaled * normed))
+    branch = input_grad * scale_v[...][None]
+    land_c[pl.ds(loc, 1)] = branch.astype(bf16)[None]
+
+    def part(low, high):
+        return lambda slot: land_c.at[slot, :, :, low:high]
+
+    low_part, high_part = part(0, cut), part(cut, model)
+    move_c = Exchange("local", locs, lambda p: low_part(loc), low_part, sems_l.at[2], sems_l.at[3])
+    move_c.start()
     move_n1.wait_recv()
     land_n2[pl.ds(loc, 1)] = jnp.sum(land_n1[...], axis=0)[None]
     move_n2 = Exchange("local", locs, lambda p: land_n2.at[loc], land_n2, sems_l.at[4], sems_l.at[5])
     move_n2.start()
-
-    move_c.wait_recv()
-    rows_x[...] = land_c[...].astype(f32).reshape(row_count, model).astype(bf16)
+    move_e = Exchange("local", locs, lambda p: high_part(loc), high_part, sems_l.at[6], sems_l.at[7])
+    move_e.start()
 
     def window_at(n):
         low = jnp.minimum((n * columns) // 128, (model - window) // 128)
         return pl.multiple_of(low * 128, 128)
 
-    move_d = Exchange(
-        "node", nodes, lambda p: rows_x.at[:, pl.ds(window_at(p), window)], land_d, sems_n.at[4], sems_n.at[5]
-    )
-    move_d.start()
-    land_d[pl.ds(node, 1)] = rows_x[:, pl.ds(window_at(node), window)][None]
+    def copy_d(target, slot, n):
+        return pltpu.make_async_remote_copy(
+            src_ref=rows_x.at[:, pl.ds(window_at(target), window)],
+            dst_ref=land_d.at[slot],
+            send_sem=sems_n.at[4, target],
+            recv_sem=sems_n.at[5, slot],
+            device_id={"node": n},
+            device_id_type=MESH,
+        )
+
+    def others(first, last, step):
+        def one(n, none):
+            @pl.when(n != node)
+            def _():
+                step(n)
+
+            return none
+
+        if last - first <= 8:
+            for n in range(first, last):
+                one(n, 0)
+        else:
+            lax.fori_loop(first, last, one, 0)
+
+    def send_columns(n):
+        copy_d(n, node, n).start()
+
+    move_c.wait_recv()
+    rows_x[:, :cut] = land_c[:, :, :, :cut].astype(f32).reshape(row_count, cut).astype(bf16)
+    others(0, early, send_columns)
 
     move_n2.wait_recv()
     land_n3[pl.ds(node, 1)] = jnp.sum(land_n2[...], axis=0)[None]
     move_n3 = Exchange("node", nodes, lambda p: land_n3.at[node], land_n3, sems_n.at[8], sems_n.at[9])
     move_n3.start()
+
+    move_e.wait_recv()
+    rows_x[:, cut:] = land_c[:, :, :, cut:].astype(f32).reshape(row_count, model - cut).astype(bf16)
+    others(early, nodes, send_columns)
+    land_d[pl.ds(node, 1)] = rows_x[:, pl.ds(window_at(node), window)][None]
 
     weight_copy.wait()
     hidden_in = lax.dot_general(
@@ -244,7 +287,7 @@
             hid_f[s, t * merge : (t + 1) * merge, :] = pre_f[at : at + merge, :]
     hid_ref[...] = hid_f[...].astype(bf16)
 
-    move_d.wait_recv()
+    others(0, nodes, lambda n: copy_d(n, n, n).wait_recv())
     move_act.wait_recv()
 
     def product(first):
@@ -272,8 +315,9 @@
         if high > low:
             norm_ref[:, low:high] = land_n3[n, :, : high - low]
 
-    for move in (move_a, move_act, move_b, move_c, move_n1, move_d, move_n2, move_n3):
+    for move in (move_a, move_act, move_b, move_c, move_e, move_n1, move_n2, move_n3):
         move.wait_send()
+    others(0, nodes, lambda n: copy_d(n, node, n).wait_send())
 
 
 def settle(*refs):
@@ -303,7 +347,10 @@
         -(-(n * columns + columns) // 128) * 128 - (n * columns) // 128 * 128 for n in range(nodes)
     )
     group = max(g for g in range(1, nodes + 1) if nodes % g == 0 and (g == 1 or g * row_count <= 512))
-    sizes = (nodes, locs, caps, merge, here, width, model, units, images, share, window, group)
+    cut = -(-model // 256) * 128
+    starts = [min(n * columns // 128, (model - window) // 128) * 128 for n in range(nodes)]
+    early = sum(1 for start in starts if start + window <= cut)
+    sizes = (nodes, locs, caps, merge, here, width, model, units, images, share, window, group, cut, early)
     f32, bf16 = jnp.float32, jnp.bfloat16
     vmem = pl.BlockSpec(memory_space=pltpu.VMEM)
     smem = pl.BlockSpec(memory_space=pltpu.SMEM)
@@ -316,7 +363,7 @@
     results = pl.pallas_call(
         functools.partial(kernel, sizes),
         out_shape=shapes,
-        in_specs=[vmem, smem, smem, vmem, anywhere, anywhere, anywhere, vmem],
+        in_specs=[anywhere, smem, smem] + [anywhere] * 5,
         out_specs=(vmem, vmem, vmem),
         scratch_shapes=[
             pltpu.SMEM((images,), jnp.int32),
@@ -343,8 +390,11 @@
             pltpu.VMEM((nodes, 2, share), f32),
             pltpu.VMEM((units, model), bf16),
             pltpu.VMEM((1, model), f32),
-            pltpu.SemaphoreType.DMA((2 + merge,)),
-            pltpu.SemaphoreType.DMA((6, locs)),
+            pltpu.VMEM(upstream.shape, bf16),
+            pltpu.VMEM((caps, width), bf16),
+            pltpu.VMEM(hidden_pre.shape, bf16),
+            pltpu.SemaphoreType.DMA((5 + merge,)),
+            pltpu.SemaphoreType.DMA((8, locs)),
             pltpu.SemaphoreType.DMA((10, nodes)),
         ],
         compiler_params=pltpu.CompilerParams(

time: 36 us -> 34.7 us (0.964)
  Pallas kernels: 35.1 us -> 33.5 us
    pallas_call x1, Pallas kernels: 32.8 us -> 31.3 us  [body(): pl.pallas_call(functools.partial(kernel, sizes), out_shape=shapes, in_spe...]
where the time goes in v4:
time: 34.7 us; the launch traced here: 34.2 us
  Pallas kernels  33.5 us (97%)
  between operations  0.64 us (2%)
    pallas_call x1, Pallas kernels, body(): pl.pallas_call(functools.partial(kernel, sizes), out_shape=shapes, in_spe...  31.3 us
    pallas_call x1, Pallas kernels, body(): pl.pallas_call(settle, out_shape=shapes, in_specs=[anywhere] * 3, out_spe...  2.28 us

profile of v4, /device:TPU:0, one launch (start us, length us, event | category | flops | bytes accessed | tf_op | source)
XLA Modules:
  0.0 34.2 jit_solution(12215418638102584950)
XLA Ops:
  0.6 31.3 %shard_map.103 = (bf16[3,16,536]{2,1,0:T(8,128)(2,1)}, f32[400,536]{1,0:T(8,128)}, f32[2,12800]{1,0:T(2,128)}) custom-call(bf16[8,12800]{1,0:T(8,128)(2,1)} %up_hbm.1, s32[64]{0:T(128)} %block_ref.1, s32[16]{0:T(128)} %owner_ref.1, bf16[3,12800]{1,0:T(4,128)(2,1)} %bitcast.3, f32[12800]{0:T(1024)} %gain_hbm.1, f32[3200]{0:T(1024)} %scale_hbm.1, ...), custom_call_target="tpu_custom_call" | custom-call | tf_op jit(solution)/shard_map/pallas_call | solution.py:363
  31.9 2.3 %shard_map.104 = (bf16[3,16,536]{2,1,0:T(8,128)(2,1)}, f32[400,536]{1,0:T(8,128)}, f32[2,12800]{1,0:T(2,128)}) custom-call(bf16[3,16,536]{2,1,0:T(8,128)(2,1)} %get-tuple-element.6.refs_0_, f32[400,536]{1,0:T(8,128)} %get-tuple-element.7.refs_1_, f32[2,12800]{1,0:T(2,128)} %get-tuple-element.8.refs_2_), custom_call_target="tpu_custom_call" | custom-call | tf_op jit(solution)/shard_map/pallas_call | solution.py:413

commit v5 on v4

--- a/solution.py
+++ b/solution.py
@@ -71,7 +71,7 @@
     hid_ref, down_ref, norm_ref,
     slot_tab, up_f, send_a, land_a, send_b, land_b, normed_f, gain_f, grad_f,
     land_c, rows_x, land_d, land_act, pre_f, deriv_f, hid_f, acc_f, terms_f, norm_s, land_n1, land_n2, land_n3,
-    weight_v, scale_v, up_ref, vis_ref, pre_ref, own_sems, sems_l, sems_n,
+    weight_v, scale_v, up_ref, vis_ref, pre_ref, hid_v, norm_v, down_v, own_sems, sems_l, sems_n,
 ):
     nodes, locs, caps, merge, here, width, model, units, images, share, window, group, cut, early = sizes
     node, loc = lax.axis_index("node"), lax.axis_index("local")
@@ -198,6 +198,20 @@
 
     grads = grad_f[...]
     normed = normed_f[...]
+    for copy in param_copies:
+        copy.wait()
+    scaled = grads * gain_f[...][None]
+    input_grad = inv_std * (scaled - mean(scaled) - normed * mean(scaled * normed))
+    branch = input_grad * scale_v[...][None]
+    land_c[pl.ds(loc, 1)] = branch.astype(bf16)[None]
+
+    def part(low, high):
+        return lambda slot: land_c.at[slot, :, :, low:high]
+
+    low_part, high_part = part(0, cut), part(cut, model)
+    move_c = Exchange("local", locs, lambda p: low_part(loc), low_part, sems_l.at[2], sems_l.at[3])
+    move_c.start()
+
     if share * nodes > width:
         terms_f[:, width:] = jnp.zeros((2, share * nodes - width), f32)
     gain_terms = jnp.sum(grads * normed, axis=0)
@@ -210,20 +224,6 @@
     move_n1 = Exchange("node", nodes, lambda p: norm_s.at[p], land_n1, sems_n.at[6], sems_n.at[7])
     move_n1.start()
     land_n1[pl.ds(node, 1)] = norm_s[pl.ds(node, 1)]
-
-    for copy in param_copies:
-        copy.wait()
-    scaled = grads * gain_f[...][None]
-    input_grad = inv_std * (scaled - mean(scaled) - normed * mean(scaled * normed))
-    branch = input_grad * scale_v[...][None]
-    land_c[pl.ds(loc, 1)] = branch.astype(bf16)[None]
-
-    def part(low, high):
-        return lambda slot: land_c.at[slot, :, :, low:high]
-
-    low_part, high_part = part(0, cut), part(cut, model)
-    move_c = Exchange("local", locs, lambda p: low_part(loc), low_part, sems_l.at[2], sems_l.at[3])
-    move_c.start()
     move_n1.wait_recv()
     land_n2[pl.ds(loc, 1)] = jnp.sum(land_n1[...], axis=0)[None]
     move_n2 = Exchange("local", locs, lambda p: land_n2.at[loc], land_n2, sems_l.at[4], sems_l.at[5])
@@ -285,7 +285,17 @@
         for s in range(caps):
             at = (t * caps + s) * merge
             hid_f[s, t * merge : (t + 1) * merge, :] = pre_f[at : at + merge, :]
-    hid_ref[...] = hid_f[...].astype(bf16)
+    hid_v[...] = hid_f[...].astype(bf16)
+    hid_copy = pltpu.make_async_copy(hid_v, hid_ref, own_sems.at[5 + merge])
+    hid_copy.start()
+
+    move_n3.wait_recv()
+    for n in range(nodes):
+        low, high = n * share, min((n + 1) * share, width)
+        if high > low:
+            norm_v[:, low:high] = land_n3[n, :, : high - low]
+    norm_copy = pltpu.make_async_copy(norm_v, norm_ref, own_sems.at[7 + merge])
+    norm_copy.start()
 
     others(0, nodes, lambda n: copy_d(n, n, n).wait_recv())
     move_act.wait_recv()
@@ -305,26 +315,42 @@
         lax.fori_loop(1, nodes // group, more, 0)
     skip = node * columns - window_at(node)
     if columns % 8 == 0:
-        down_ref[...] = acc_f[pl.ds(pl.multiple_of(skip, 8), columns), :]
+        result = acc_f.at[pl.ds(pl.multiple_of(skip, 8), columns)]
     else:
-        down_ref[...] = pltpu.roll(acc_f[...], lax.rem(window - skip, window), 0)[:columns, :]
-
-    move_n3.wait_recv()
-    for n in range(nodes):
-        low, high = n * share, min((n + 1) * share, width)
-        if high > low:
-            norm_ref[:, low:high] = land_n3[n, :, : high - low]
+        down_v[...] = pltpu.roll(acc_f[...], lax.rem(window - skip, window), 0)[:columns, :]
+        result = down_v
+    down_copy = pltpu.make_async_copy(result, down_ref, own_sems.at[6 + merge])
+    down_copy.start()
 
     for move in (move_a, move_act, move_b, move_c, move_e, move_n1, move_n2, move_n3):
         move.wait_send()
     others(0, nodes, lambda n: copy_d(n, node, n).wait_send())
+    for copy in (hid_copy, norm_copy, down_copy):
+        copy.wait()
 
 
 def settle(*refs):
-    copies = [pltpu.make_async_copy(refs[i], refs[3 + i], refs[6].at[i]) for i in range(3)]
-    for copy in copies:
+    ins, outs, held, arrive, leave = refs[:3], refs[3:6], refs[6:9], refs[9], refs[10]
+    copies = []
+    for i in range(3):
+        rows = ins[i].shape[0]
+        step = -(-rows // 32) * 8 if rows > 64 else rows
+        for low in range(0, rows, step):
+            copies.append((i, slice(low, min(low + step, rows))))
+    inward = [
+        pltpu.make_async_copy(ins[i].at[part], held[i].at[part], arrive.at[c])
+        for c, (i, part) in enumerate(copies)
+    ]
+    outward = [
+        pltpu.make_async_copy(held[i].at[part], outs[i].at[part], leave.at[c])
+        for c, (i, part) in enumerate(copies)
+    ]
+    for copy in inward:
         copy.start()
-    for copy in copies:
+    for c in range(len(copies)):
+        inward[c].wait()
+        outward[c].start()
+    for copy in outward:
         copy.wait()
 
 
@@ -364,7 +390,7 @@
         functools.partial(kernel, sizes),
         out_shape=shapes,
         in_specs=[anywhere, smem, smem] + [anywhere] * 5,
-        out_specs=(vmem, vmem, vmem),
+        out_specs=(anywhere,) * 3,
         scratch_shapes=[
             pltpu.SMEM((images,), jnp.int32),
             pltpu.VMEM((locs, here * merge, model), f32),
@@ -393,7 +419,10 @@
             pltpu.VMEM(upstream.shape, bf16),
             pltpu.VMEM((caps, width), bf16),
             pltpu.VMEM(hidden_pre.shape, bf16),
-            pltpu.SemaphoreType.DMA((5 + merge,)),
+            pltpu.VMEM(hidden_pre.shape, bf16),
+            pltpu.VMEM((2, width), f32),
+            pltpu.VMEM((columns, units) if columns % 8 else (8, 128), f32),
+            pltpu.SemaphoreType.DMA((8 + merge,)),
             pltpu.SemaphoreType.DMA((8, locs)),
             pltpu.SemaphoreType.DMA((10, nodes)),
         ],
@@ -414,8 +443,9 @@
         settle,
         out_shape=shapes,
         in_specs=[anywhere] * 3,
-        out_specs=(vmem,) * 3,
-        scratch_shapes=[pltpu.SemaphoreType.DMA((3,))],
+        out_specs=(anywhere,) * 3,
+        scratch_shapes=[pltpu.VMEM(shape.shape, shape.dtype) for shape in shapes]
+        + [pltpu.SemaphoreType.DMA((16,)), pltpu.SemaphoreType.DMA((16,))],
         compiler_params=pltpu.CompilerParams(vmem_limit_bytes=56 * 1024 * 1024),
     )(*results)
 

time: 34.7 us -> 34.7 us (level)
  the two profiles are of different devices: /device:TPU:0 before, /device:TPU:5 now
where the time goes in v5:
time: 34.7 us; the launch traced here: 34.5 us
  Pallas kernels  33.9 us (98%)
  between operations  0.64 us (2%)
    pallas_call x1, Pallas kernels, body(): pl.pallas_call(functools.partial(kernel, sizes), out_shape=shapes, in_spe...  31.7 us
    pallas_call x1, Pallas kernels, body(): pl.pallas_call(settle, out_shape=shapes, in_specs=[anywhere] * 3, out_spe...  2.25 us

profile of v5, /device:TPU:5, one launch (start us, length us, event | category | flops | bytes accessed | tf_op | source)
XLA Modules:
  0.0 34.5 jit_solution(18186535630733706619)
XLA Ops:
  0.6 31.7 %shard_map.103 = (bf16[3,16,536]{2,1,0:T(8,128)(2,1)}, f32[400,536]{1,0:T(8,128)}, f32[2,12800]{1,0:T(2,128)}) custom-call(bf16[8,12800]{1,0:T(8,128)(2,1)} %up_hbm.1, s32[64]{0:T(128)} %block_ref.1, s32[16]{0:T(128)} %owner_ref.1, bf16[3,12800]{1,0:T(4,128)(2,1)} %bitcast.3, f32[12800]{0:T(1024)} %gain_hbm.1, f32[3200]{0:T(1024)} %scale_hbm.1, ...), custom_call_target="tpu_custom_call" | custom-call | tf_op jit(solution)/shard_map/pallas_call | solution.py:389
  32.3 2.3 %shard_map.104 = (bf16[3,16,536]{2,1,0:T(8,128)(2,1)}, f32[400,536]{1,0:T(8,128)}, f32[2,12800]{1,0:T(2,128)}) custom-call(bf16[3,16,536]{2,1,0:T(8,128)(2,1)} %get-tuple-element.6.refs_0_, f32[400,536]{1,0:T(8,128)} %get-tuple-element.7.refs_1_, f32[2,12800]{1,0:T(2,128)} %get-tuple-element.8.refs_2_), custom_call_target="tpu_custom_call" | custom-call | tf_op jit(solution)/shard_map/pallas_call | solution.py:442
